TPU v7x, 32 devices: a whole 2x2x4 slice. The times are simulated.
32 devices in a mesh: rep: 4 (over x, core), shard: 8 (over z, y).
Axes of the slice: x: 2, y: 2, z: 4, core: 2. Of those that a mesh axis runs over, the one named last changes fastest.
Arguments:
- tokens_in: bfloat16 [16384, 8192], P(('rep', 'shard'))
- key_cotangent: bfloat16 [16384, 1024], P(('rep', 'shard'))
- token_counts: int32 [4, 32], P(None, ('rep', 'shard')), may hold values from 128 to 512, as said below
- grad_accum: float32 [8192, 1024], P('shard')
- key_weight: float32 [8192, 1024], P('shard')
- row_moment: float32 [8192], P('shard'), may hold values from 0.1 to 0.3
- col_moment: float32 [1024], replicated, may hold values from 0.0001 to 0.001
Outputs:
- new_weight: float32 [8192, 1024], P('shard')
- direction: float32 [8192, 1024], P('shard')
- new_row: float32 [8192], P('shard')
- new_col: float32 [1024], replicated
Inputs may be any that keep to these rules, and one draw needn't show every extreme that they name: Column d of token_counts belongs to device d in the order rep, then shard; the live tokens of the last microbatch are the first token_counts[3, d] of that device's 512 slots. Some entry equals 512 and some equals 128.
All inputs are finite; a program needn't handle non-finite values.
Results may differ from a plain program's by a relative error of at most 0.0003.
Values may be sent and summed in bfloat16 or wider, within the bound.
A program may use at most 128 MiB of HBM per device.

v0:
```python
import jax
import jax.numpy as jnp
from jax import lax
from jax.sharding import PartitionSpec as P

D = 8192
KV = 1024


eps_square = 1e-30
decay_rate = 0.6
clip_bound = 1.0
step_rate = 0.05


def adapt(grad_sum, accum, weight, old_row, old_col, total):
    entries = D * KV
    grad = (accum + grad_sum) / total
    grad_sq = grad * grad
    squares = grad_sq + eps_square
    new_row = decay_rate * old_row + (1.0 - decay_rate) * jnp.mean(squares, axis=1)
    col_part = jnp.sum(squares, axis=0)
    weight_part = jnp.sum(weight * weight)
    col_sum, weight_sum = lax.psum((col_part, weight_part), "shard")
    new_col = decay_rate * old_col + (1.0 - decay_rate) * (col_sum / D)
    update = grad * lax.rsqrt(new_row[:, None] * new_col[None, :])
    update_sq = lax.psum(jnp.sum(update * update), "shard")
    clip = jnp.maximum(1.0, jnp.sqrt(update_sq / entries) / clip_bound)
    direction = update / clip
    weight_rms = jnp.sqrt(weight_sum / entries)
    new_weight = weight - step_rate * weight_rms * direction
    return (new_weight, direction, new_row, new_col)


def body(tokens_in, key_cotangent, token_counts, grad_accum, key_weight, row_moment, col_moment):
    slots = tokens_in.shape[0]
    count_sum = lax.psum(jnp.sum(token_counts), ("rep", "shard"))
    total = count_sum.astype(jnp.float32)
    live = token_counts[token_counts.shape[0] - 1, 0]
    keep = lax.broadcasted_iota(jnp.int32, (slots, 1), 0) < live
    masked = jnp.where(keep, key_cotangent, jnp.zeros((), key_cotangent.dtype))
    columns = lax.all_to_all(tokens_in, "shard", split_axis=1, concat_axis=0, tiled=True)
    last_grad = lax.dot_general(
        columns,
        lax.all_gather(masked, "shard", axis=0, tiled=True),
        (((0,), (0,)), ((), ())),
        preferred_element_type=jnp.float32,
    )
    whole = lax.psum(last_grad, "rep")
    return adapt(whole, grad_accum, key_weight, row_moment, col_moment, total)


def solution(mesh):
    in_specs = (
        P(("rep", "shard"), None),
        P(("rep", "shard"), None),
        P(None, ("rep", "shard")),
        P("shard", None),
        P("shard", None),
        P("shard"),
        P(),
    )
    out_specs = (P("shard", None), P("shard", None), P("shard"), P())
    return jax.shard_map(body, mesh=mesh, in_specs=in_specs, out_specs=out_specs, check_vma=False)
```

profile of v0, /device:TPU:0, one launch (start us, length us, event | category | flops | bytes accessed | tf_op | source)
XLA Modules:
  0.0 505.3 jit_solution(3351235293307568425)
XLA Ops:
  7.2 12.0 %copy.19 = bf16[512,8192]{0,1:T(8,128)(2,1)} copy(bf16[512,8192]{1,0:T(8,128)(2,1)} %param.7) | data formatting | bytes 16777216 | tf_op args[0]
  19.1 7.4 %all-to-all-start = ((bf16[512,8,1024]{0,2,1:T(8,128)(2,1)}), bf16[512,8,1024]{0,2,1:T(8,128)(2,1)}, u32[]{:S(2)}, u32[]{:S(2)}) async-start(bf16[512,8,1024]{0,2,1:T(8,128)(2,1)} %bitcast.8), calls=%async_computation | async-start | bytes 16777216 | tf_op jit(solution)/shard_map/all_to_all | solution.py:42
  26.5 0.0 all-gather.2.cloned.1.call-start
  26.6 0.0 copy-done.5
  26.6 0.6 slice.3
  27.2 0.6 iota_compare_fusion
  27.8 0.0 copy-done
  27.8 1.1 broadcast_select_fusion
  29.0 0.0 all-gather.2.cloned.1.call-update
  29.0 0.0 all-reduce.3.cloned.1.call-start
  29.0 282.0 %all-to-all-done = bf16[512,8,1024]{0,2,1:T(8,128)(2,1)} async-done(((bf16[512,8,1024]{0,2,1:T(8,128)(2,1)}), bf16[512,8,1024]{0,2,1:T(8,128)(2,1)}, u32[]{:S(2)}, u32[]{:S(2)}) %all-to-all-start) | async-done | bytes 8388640 | tf_op jit(solution)/shard_map/all_to_all | solution.py:42
  311.0 11.5 %copy.20 = bf16[8,512,1024]{2,1,0:T(8,128)(2,1)} copy(bf16[8,512,1024]{1,2,0:T(8,128)(2,1)} %bitcast.2) | data formatting | bytes 16777216 | tf_op jit(solution)/shard_map/all_to_all | solution.py:42
  322.5 15.0 %convolution_bitcast_fusion = f32[1024,1024]{0,1:T(8,128)} fusion(bf16[4096,1024]{1,0:T(8,128)(2,1)} %all-gather.2.cloned.1.call-done, bf16[4096,1024]{1,0:T(8,128)(2,1)} %bitcast.9), kind=kOutput, calls=%fused_computation.9 | convolution fusion | flops 8589934592 | bytes 20971520 | tf_op jit(solution)/shard_map/dot_general | solution.py:43
  337.5 0.0 all-reduce.3.cloned.1.call-update
  337.6 0.6 reduce_sum.46
  338.2 38.6 %psum.37 = s32[]{:T(128)} all-reduce(s32[]{:T(128)} %reduce_sum.46), channel_id=1, replica_groups=mesh['rep'=4,'shard'=8] {'rep','shard'}, use_global_device_ids=true, to_apply=%region_4.5 | all-reduce | flops 1 | bytes 8 | tf_op jit(solution)/shard_map/psum | solution.py:37
  376.8 5.4 %copy.21 = f32[1024,1024]{0,1:T(8,128)} copy(f32[1024,1024]{1,0:T(8,128)} %param.10) | data formatting | bytes 8388608 | tf_op args[3]
  382.9 3.9 multiply_reduce_fusion.1
  386.7 36.3 %all-reduce.3.cloned.1.call-done = f32[1024,1024]{0,1:T(8,128)} async-done(((f32[1024,1024]{0,1:T(8,128)}), f32[1024,1024]{0,1:T(8,128)}) %all-reduce.3.cloned.1.call-update) | async-done | bytes 4194320 | tf_op jit(solution)/shard_map/psum | solution.py:49
  423.1 6.6 %fusion.1 = (f32[1024]{0:T(1024)S(1)}, f32[1024]{0:T(1024)S(1)}, f32[1024,1024]{0,1:T(8,128)}) fusion(f32[]{:T(128)S(6)} %convert_element_type.3, f32[1024,1024]{0,1:T(8,128)} %copy.21, f32[1024,1024]{0,1:T(8,128)} %all-reduce.3.cloned.1.call-done), kind=kLoop, calls=%fused_computation.7 | loop fusion | flops 6289408 | bytes 12591108 | tf_op jit(solution)/shard_map/reduce_sum | solution.py:21
  429.6 21.4 %psum.38 = f32[1024]{0:T(1024)S(1)} all-reduce(f32[1024]{0:T(1024)S(1)} %get-tuple-element.17), channel_id=1, replica_groups=mesh['rep'=4,'shard'=8] {'shard'}, use_global_device_ids=true, to_apply=%region_7.8 | all-reduce | flops 1024 | bytes 8192 | tf_op jit(solution)/shard_map/psum | solution.py:24
  451.0 0.0 copy-done.3
  451.0 0.0 copy-start.1
  451.1 0.0 copy-start.2
  451.1 4.3 multiply_reduce_fusion
  455.4 5.3 %copy.22 = f32[1024,1024]{0,1:T(8,128)} copy(f32[1024,1024]{1,0:T(8,128)} %param.11) | data formatting | bytes 8388608 | tf_op args[4]
  460.7 17.8 %all-reduce = (f32[]{:T(128)}, f32[]{:T(128)}) all-reduce(f32[]{:T(128)} %multiply_reduce_fusion, f32[]{:T(128)} %multiply_reduce_fusion.1), channel_id=1, replica_groups=mesh['rep'=4,'shard'=8] {'shard'}, use_global_device_ids=true, to_apply=%region_9.10 | all-reduce | flops 2 | bytes 16 | tf_op jit(solution)/shard_map/psum | solution.py:27
  479.9 0.0 copy-done.1
  479.9 0.0 copy-done.2
  480.0 7.8 %multiply_subtract_fusion = (f32[1024,1024]{0,1:T(8,128)}, f32[1024,1024]{0,1:T(8,128)}) fusion(f32[1024,1024]{0,1:T(8,128)} %copy.22, f32[]{:T(128)S(6)} %mul_shard_map.3, f32[]{:T(128)S(6)} %max.3, f32[1024,1024]{0,1:T(8,128)} %get-tuple-element.22, f32[1024]{0:T(1024)S(1)} %multiply_add_fusion.1, f32[1024]{0:T(1024)S(1)} %multiply_add_fusion.2), kind=kLoop, calls=%fused_computation | loop fusion | flops 5242880 | bytes 16785416 | tf_op jit(solution)/shard_map/sub | solution.py:31
  487.8 5.3 %copy.23 = f32[1024,1024]{1,0:T(8,128)} copy(f32[1024,1024]{0,1:T(8,128)} %get-tuple-element.20) | data formatting | bytes 8388608
  493.1 5.3 %copy.24 = f32[1024,1024]{1,0:T(8,128)} copy(f32[1024,1024]{0,1:T(8,128)} %get-tuple-element.21) | data formatting | bytes 8388608
  (8 shorter events, 0.0 us)
Async XLA Ops:
  19.1 7.5 %copy-start.5 = (s32[4,1]{0,1:T(1,128)S(1)}, s32[4,1]{0,1:T(1,128)}, u32[]{:S(2)}) copy-start(s32[4,1]{0,1:T(1,128)} %param.9) | copy-start | bytes 52
  19.1 8.7 %copy-start = (bf16[512,1024]{1,0:T(8,128)(2,1)S(1)}, bf16[512,1024]{1,0:T(8,128)(2,1)}, u32[]{:S(2)}) copy-start(bf16[512,1024]{1,0:T(8,128)(2,1)} %param.8) | copy-start | bytes 3145732
  19.1 291.9 %all-to-all-start = ((bf16[512,8,1024]{0,2,1:T(8,128)(2,1)}), bf16[512,8,1024]{0,2,1:T(8,128)(2,1)}, u32[]{:S(2)}, u32[]{:S(2)}) async-start(bf16[512,8,1024]{0,2,1:T(8,128)(2,1)} %bitcast.8), calls=%async_computation | async-start | bytes 16777216 | tf_op jit(solution)/shard_map/all_to_all | solution.py:42
  26.5 296.0 %all-gather.2.cloned.1.call-start = ((), (), s32[]{:S(2)}) async-start(), calls=%async_computation.1 | async-start | bytes 9437184 | tf_op jit(solution)/shard_map/all_gather | solution.py:45
  29.0 394.1 %all-reduce.3.cloned.1.call-start = ((), (), s32[]{:S(2)}) async-start(), calls=%async_computation.2 | async-start | bytes 8388608 | tf_op jit(solution)/shard_map/psum | solution.py:49
  386.7 64.3 %copy-start.3 = (f32[1024]{0:T(1024)S(1)}, f32[1024]{0:T(1024)}, u32[]{:S(2)}) copy-start(f32[1024]{0:T(1024)} %param.13) | copy-start | bytes 12292
  386.7 64.3 %copy-start.4 = (f32[1024]{0:T(1024)S(1)}, f32[1024]{0:T(1024)}, u32[]{:S(2)}) copy-start(f32[1024]{0:T(1024)} %param.12) | copy-start | bytes 12292
  451.0 28.9 %copy-start.1 = (f32[1024]{0:T(1024)}, f32[1024]{0:T(1024)S(1)}, u32[]{:S(2)}) copy-start(f32[1024]{0:T(1024)S(1)} %multiply_add_fusion.1) | copy-start | bytes 12292
  451.1 28.9 %copy-start.2 = (f32[1024]{0:T(1024)}, f32[1024]{0:T(1024)S(1)}, u32[]{:S(2)}) copy-start(f32[1024]{0:T(1024)S(1)} %multiply_add_fusion.2) | copy-start | bytes 12292
Sparse Core Ops, SparseCore 0:
  30.1 271.1 all-gather.1
  337.7 85.3 all-reduce.2
where the time goes:
time: 506 us; the launch traced here: 505 us
  waiting for transfers between devices  318 us (63%)
  blocking collectives  77.8 us (15%)
  local copies, waits for them, and re-layouts  45.5 us (9%)
  other arithmetic  25 us (5%)
  between operations  16.2 us (3%)
  matrix products  15 us (3%)
  starting transfers between devices  7.49 us (1%)
    all_to_all x1, waiting for transfers between devices, body(): lax.all_to_all(tokens_in, 'shard', split_axis=1, concat_axis=0, tiled=True)  282 us
    psum x1, blocking collectives, body(): count_sum = lax.psum(jnp.sum(token_counts), ('rep', 'shard'))  38.6 us
    psum x1, waiting for transfers between devices, body(): whole = lax.psum(last_grad, 'rep')  36.3 us
    unnamed x17, local copies, waits for them, and re-layouts  33.4 us
    psum x1, blocking collectives, adapt(): col_sum, weight_sum = lax.psum((col_part, weight_part), 'shard')  21.4 us
    psum x1, blocking collectives, adapt(): update_sq = lax.psum(jnp.sum(update * update), 'shard')  17.8 us
    dot_general x1, matrix products, body(): lax.dot_general(columns, lax.all_gather(masked, 'shard', axis=0, tiled=Tr...  15 us
    all_to_all x1, local copies, waits for them, and re-layouts, body(): lax.all_to_all(tokens_in, 'shard', split_axis=1, concat_axis=0, tiled=True)  11.5 us
  transfers between devices with their start and end apart: 3, of which 2 were waited for; matrix products, arithmetic and copies ran while one was open for 5% of the time, Pallas kernels for 0%

commit v1 on v0

v1 whole, which is shorter than its diff:
```python
import functools

import jax
import jax.numpy as jnp
from jax import lax
from jax.experimental import pallas as pl
from jax.experimental.pallas import tpu as pltpu
from jax.sharding import PartitionSpec as P

EPS = 1e-30
DECAY = 0.6
CLIP = 1.0
RATE = 0.05
MESH = pl.DeviceIdType.MESH
WINDOW = 3
F32 = jnp.float32


def lo_size(shard):
    return 2 if shard == 8 else 4


def kernel(dims, t_ref, k_ref, cnt_ref, acc_ref, w_ref, row_ref, g_out, s_out,
           t_buf, k_buf, part, y_buf, z_buf, acc_v, w_v, row_v, g_buf,
           c1, c2, c3, s1, s2, s3,
           t_local, t_send, t_recv, k_local, kx_send, kx_recv, kc_send, kc_recv,
           kf_send, kf_recv, y_send, y_recv, z_send, z_recv, in_sem,
           g_local, gx_send, gx_recv, gc_send, gc_recv, gf_send, gf_recv,
           a_send, a_recv, b_send, b_recv):
    R, S, H, L, G, sub, tok, natural = dims
    X = R // 2
    NG = L // G
    NCH = H * NG
    width = G * sub
    D = S * R * sub
    rep, shard = lax.axis_index("rep"), lax.axis_index("shard")
    x, c = rep // 2, rep % 2
    sib = x * 2 + (1 - c)
    hi, lo = shard // L, shard % L
    g0 = lo // G

    def dev_rep(r):
        return (r, shard)

    def dev_lo(l):
        return (rep, hi * L + l)

    def dev_hi(h):
        return (rep, h * L + lo)

    def rcopy(src, dst, ss, rs, dev):
        return pltpu.make_async_remote_copy(src_ref=src, dst_ref=dst, send_sem=ss, recv_sem=rs,
                                            device_id=dev, device_id_type=MESH)

    barrier = pltpu.get_barrier_semaphore()
    peers = ([dev_rep((rep + p) % R) for p in range(1, R)] + [dev_lo((lo + p) % L) for p in range(1, L)]
             + [dev_hi((hi + p) % H) for p in range(1, H)])
    for dev in peers:
        pl.semaphore_signal(barrier, inc=1, device_id=dev, device_id_type=MESH)
    in_copies = []
    rows = pl.ds(pl.multiple_of(rep * sub, sub), sub)
    for i, (src, dst) in enumerate(((acc_ref, acc_v), (w_ref, w_v), (row_ref, row_v))):
        cp = pltpu.make_async_copy(src.at[rows], dst, in_sem.at[i])
        cp.start()
        in_copies.append(cp)
    my_tok = pl.ds(pl.multiple_of(rep * tok, tok), tok)
    k_cp = pltpu.make_async_copy(k_ref, k_buf.at[my_tok], k_local.at[0])
    k_cp.start()
    pl.semaphore_wait(barrier, len(peers))

    def reduce_all(first, b1, b2, b3, sends, recvs):
        value = first
        base = 0
        for buf, n, me, dev in ((b1, R, rep, dev_rep), (b2, L, lo, dev_lo), (b3, H, hi, dev_hi)):
            buf[me] = value
            cps = []
            for p in range(1, n):
                cp = rcopy(buf.at[me], buf.at[me], sends.at[base + p - 1], recvs.at[base + p - 1], dev((me + p) % n))
                cp.start()
                cps.append(cp)
            for cp in cps:
                cp.wait_send()
                cp.wait_recv()
            base += n - 1
            value = buf[0]
            for i in range(1, n):
                value = value + buf[i]
        return value

    k_sib = rcopy(k_ref, k_buf.at[my_tok], kc_send.at[0], kc_recv.at[0], dev_rep(sib))
    k_far = [rcopy(k_ref, k_buf.at[my_tok], kx_send.at[q - 1], kx_recv.at[q - 1],
                   dev_rep(((x + q) % X) * 2 + c)) for q in range(1, X)]
    for cp in k_far:
        cp.start()
    k_sib.start()

    def k_fwd(q):
        src = ((x + X - q) % X) * 2 + c
        at = pl.ds(pl.multiple_of(src * tok, tok), tok)
        return rcopy(k_buf.at[at], k_buf.at[at], kf_send.at[q - 1], kf_recv.at[q - 1], dev_rep(sib))

    def block_of(t):
        return ((hi + 1 + t // NG) % H) * L + ((g0 + 1 + t % NG) % NG) * G

    def t_cols(r, s0):
        if natural:
            off = s0 * (R * sub) + r * sub
        else:
            off = r * (S * sub) + s0 * sub
        return pl.ds(pl.multiple_of(off, width), width)

    def t_dst(s0):
        return t_buf.at[my_tok, pl.ds(pl.multiple_of(s0 * sub, width), width)]

    def t_loc(t):
        s0 = block_of(t)
        return pltpu.make_async_copy(t_ref.at[:, t_cols(rep, s0)], t_dst(s0), t_local.at[t])

    def t_rem(t, p):
        s0 = block_of(t)
        to = (rep + p) % R
        return rcopy(t_ref.at[:, t_cols(to, s0)], t_dst(s0), t_send.at[p - 1, t], t_recv.at[p - 1, t], dev_rep(to))

    def t_start(t):
        for p in range(1, R):
            t_rem(t, p).start()
        t_loc(t).start()

    for t in range(min(WINDOW, NCH)):
        t_start(t)

    total = reduce_all(cnt_ref[...], c1, c2, c3, a_send, a_recv)

    for q in range(1, X):
        k_far[q - 1].wait_recv()
        k_fwd(q).start()
    k_cp.wait()
    k_sib.wait_recv()
    for q in range(1, X):
        k_fwd(q).wait_recv()

    def part_rows(s, n=1):
        return pl.ds(pl.multiple_of(s * sub, n * sub), n * sub)

    def y_copy(k, lt, p):
        s = ((hi + 1 + k) % H) * L + lt
        return rcopy(part.at[part_rows(s)], y_buf.at[p - 1, k], y_send.at[p - 1, k], y_recv.at[p - 1, k], dev_lo(lt))

    def z_copy(k):
        h = (hi + 1 + k) % H
        return rcopy(part.at[part_rows(h * L + lo)], z_buf.at[k], z_send.at[k], z_recv.at[k], dev_hi(h))

    def y_add(k):
        s = ((hi + 1 + k) % H) * L + lo
        at = part_rows(s)
        for p in range(1, L):
            y_copy(k, (lo + p) % L, p).wait_recv()
        value = part[at, :]
        for p in range(1, L):
            value = value + y_buf[p - 1, k]
        part[at, :] = value

    def step(k, carry):
        for j in range(NG):
            t = k * NG + j
            t_loc(t).wait()
            for p in range(1, R):
                t_rem(t, p).wait_recv()

            @pl.when(t + WINDOW < NCH)
            def _():
                t_start(t + WINDOW)

            s0 = block_of(t)
            at = pl.ds(pl.multiple_of(s0 * sub, width), width)
            part[at, :] = lax.dot_general(t_buf[:, at], k_buf[...], (((0,), (0,)), ((), ())),
                                          preferred_element_type=F32)
            for i in range(G):
                lt = s0 % L + i
                p = (lt - lo + L) % L
                if G == 1:
                    if j < NG - 1:
                        y_copy(k, lt, p).start()
                else:
                    @pl.when(p > 0)
                    def _():
                        y_copy(k, lt, p).start()
            if j == 0:
                @pl.when(k > 0)
                def _():
                    y_add(k - 1)
                    z_copy(k - 1).start()
        return carry

    lax.fori_loop(0, H, step, 0)
    y_add(H - 1)
    for k in range(H - 1):
        z_copy(k).wait_recv()
    for cp in in_copies:
        cp.wait()
    value = part[part_rows(shard), :]
    for k in range(H - 1):
        value = value + z_buf[k]
    grad = (acc_v[...] + value) / total[0:1, 0:1]
    g_buf[:, :acc_v.shape[1]] = grad
    g2 = grad * grad
    squares = g2 + EPS
    mean = jnp.sum(squares, axis=1, keepdims=True) / squares.shape[1]
    new_row = DECAY * row_v[...] + (1.0 - DECAY) * mean
    g_buf[:, acc_v.shape[1]:] = new_row

    g_cp = pltpu.make_async_copy(g_buf, g_out.at[rows], g_local.at[0])
    g_sib = rcopy(g_buf, g_out.at[rows], gc_send.at[0], gc_recv.at[0], dev_rep(sib))
    g_far = [rcopy(g_buf, g_out.at[rows], gx_send.at[q - 1], gx_recv.at[q - 1],
                   dev_rep(((x + q) % X) * 2 + c)) for q in range(1, X)]
    for cp in g_far:
        cp.start()
    g_sib.start()
    g_cp.start()

    col = jnp.sum(squares, axis=0, keepdims=True)
    upd = jnp.sum(g2 * (1.0 / new_row[:, :1]), axis=0, keepdims=True)
    w = w_v[...]
    wsq = jnp.sum(w * w, axis=0, keepdims=True)
    stats = jnp.concatenate([col, upd, wsq, jnp.zeros((5, col.shape[1]), F32)], axis=0)
    s_out[...] = reduce_all(stats, s1, s2, s3, b_send, b_recv)

    def g_fwd(q):
        src = ((x + X - q) % X) * 2 + c
        at = pl.ds(pl.multiple_of(src * sub, sub), sub)
        return rcopy(g_out.at[at], g_out.at[at], gf_send.at[q - 1], gf_recv.at[q - 1], dev_rep(sib))

    for q in range(1, X):
        g_far[q - 1].wait_recv()
        g_fwd(q).start()
    g_cp.wait()
    g_sib.wait()

    k_sib.wait_send()
    for q in range(1, X):
        k_far[q - 1].wait_send()
        k_fwd(q).wait_send()
        g_far[q - 1].wait_send()
        g_fwd(q).wait()

    def t_done(t, carry):
        for p in range(1, R):
            t_rem(t, p).wait_send()
        return carry

    lax.fori_loop(0, NCH, t_done, 0)
    for k in range(H):
        for p in range(1, L):
            y_copy(k, (lo + p) % L, p).wait_send()
        if k < H - 1:
            z_copy(k).wait_send()


def body(R, S, L, tokens_in, key_cotangent, token_counts, grad_accum, key_weight, row_moment, col_moment):
    tok, D = tokens_in.shape
    KV = key_cotangent.shape[1]
    H = S // L
    sub = D // (R * S)
    B = R * sub
    X = R // 2
    natural = sub % 128 == 0
    G = 1 if natural else 128 // sub
    NCH = S // G
    live = token_counts[token_counts.shape[0] - 1, 0]
    keep = lax.broadcasted_iota(jnp.int32, (tok, 1), 0) < live
    masked = jnp.where(keep, key_cotangent, jnp.zeros((), key_cotangent.dtype))
    count = jnp.full((8, 128), jnp.sum(token_counts).astype(F32))
    rows = jnp.broadcast_to(row_moment[:, None], (B, 128))
    tokens = tokens_in
    if not natural:
        tokens = tokens.reshape(tok, S, R, sub).transpose(0, 2, 1, 3).reshape(tok, D)
    dims = (R, S, H, L, G, sub, tok, natural)
    any_spec = pl.BlockSpec(memory_space=pl.ANY)
    vmem = pl.BlockSpec(memory_space=pltpu.VMEM)
    dma = pltpu.SemaphoreType.DMA
    n_all = (R - 1) + (L - 1) + (H - 1)
    X1 = max(X - 1, 1)
    grads, stats = pl.pallas_call(
        functools.partial(kernel, dims),
        out_shape=(jax.ShapeDtypeStruct((B, KV + 128), F32), jax.ShapeDtypeStruct((8, KV), F32)),
        in_specs=[any_spec, any_spec, vmem, any_spec, any_spec, any_spec],
        out_specs=(any_spec, vmem),
        scratch_shapes=[
            pltpu.VMEM((R * tok, S * sub), jnp.bfloat16),
            pltpu.VMEM((R * tok, KV), jnp.bfloat16),
            pltpu.VMEM((S * sub, KV), F32),
            pltpu.VMEM((L - 1, H, sub, KV), F32),
            pltpu.VMEM((H - 1, sub, KV), F32),
            pltpu.VMEM((sub, KV), F32),
            pltpu.VMEM((sub, KV), F32),
            pltpu.VMEM((sub, 128), F32),
            pltpu.VMEM((sub, KV + 128), F32),
            pltpu.VMEM((R, 8, 128), F32),
            pltpu.VMEM((L, 8, 128), F32),
            pltpu.VMEM((H, 8, 128), F32),
            pltpu.VMEM((R, 8, KV), F32),
            pltpu.VMEM((L, 8, KV), F32),
            pltpu.VMEM((H, 8, KV), F32),
            dma((NCH,)), dma((R - 1, NCH)), dma((R - 1, NCH)),
            dma((1,)), dma((X1,)), dma((X1,)), dma((1,)), dma((1,)), dma((X1,)), dma((X1,)),
            dma((L - 1, H)), dma((L - 1, H)), dma((H - 1,)), dma((H - 1,)),
            dma((3,)),
            dma((1,)), dma((X1,)), dma((X1,)), dma((1,)), dma((1,)), dma((X1,)), dma((X1,)),
            dma((n_all,)), dma((n_all,)), dma((n_all,)), dma((n_all,)),
        ],
        compiler_params=pltpu.CompilerParams(collective_id=0, has_side_effects=True,
                                             vmem_limit_bytes=50 * 1024 * 1024),
        cost_estimate=pl.CostEstimate(flops=2 * tok * D * KV, bytes_accessed=24 * 1024 * 1024, transcendentals=0),
    )(tokens, masked, count, grad_accum, key_weight, rows)
    entries = D * KV
    new_col = DECAY * col_moment + (1.0 - DECAY) * (stats[0] / D)
    update_sq = jnp.sum(stats[1] / new_col)
    weight_sum = jnp.sum(stats[2])
    new_row = grads[:, KV]
    clip = jnp.maximum(1.0, jnp.sqrt(update_sq / entries) / CLIP)
    direction = grads[:, :KV] * lax.rsqrt(new_row[:, None] * new_col[None, :]) / clip
    weight_rms = jnp.sqrt(weight_sum / entries)
    new_weight = key_weight - RATE * weight_rms * direction
    return (new_weight, direction, new_row, new_col)


def solution(mesh):
    R, S = mesh.shape["rep"], mesh.shape["shard"]
    in_specs = (
        P(("rep", "shard"), None),
        P(("rep", "shard"), None),
        P(None, ("rep", "shard")),
        P("shard", None),
        P("shard", None),
        P("shard"),
        P(),
    )
    out_specs = (P("shard", None), P("shard", None), P("shard"), P())
    return jax.shard_map(functools.partial(body, R, S, lo_size(S)), mesh=mesh, in_specs=in_specs,
                         out_specs=out_specs, check_vma=False)
```

time: 506 us -> 244 us (0.48)
  waiting for transfers between devices: 318 us -> 0 us
  Pallas kernels: 0 us -> 227 us
  blocking collectives: 77.8 us -> 0 us
  local copies, waits for them, and re-layouts: 45.5 us -> 3.38 us
  matrix products: 15 us -> 0 us
  other arithmetic: 25 us -> 10.7 us
  between operations: 16.2 us -> 2.74 us
  starting transfers between devices: 7.49 us -> 0 us
    all_to_all x1 -> x0, waiting for transfers between devices: 282 us -> none  [body(): lax.all_to_all(tokens_in, 'shard', split_axis=1, concat_axis=0, tiled=True)]
    pallas_call x0 -> x1, Pallas kernels: none -> 227 us  [body(): pl.pallas_call(functools.partial(kernel, dims), out_shape=(jax.ShapeDtype...]
    psum x3 -> x0, blocking collectives: 77.8 us -> none  [the longest x1 38.6 us: body(): count_sum = lax.psum(jnp.sum(token_counts), ('rep', 'shard'))]
    psum x1 -> x0, waiting for transfers between devices: 36.3 us -> none  [body(): whole = lax.psum(last_grad, 'rep')]
    unnamed x17 -> x6, local copies, waits for them, and re-layouts: 33.4 us -> 0.02 us
    dot_general x1 -> x0, matrix products: 15 us -> none  [body(): lax.dot_general(columns, lax.all_gather(masked, 'shard', axis=0, tiled=Tr...]
    reduce_sum x4 -> x2, other arithmetic: 15.4 us -> 1.9 us  [the longest x1 1.3 us: body(): count = jnp.full((8, 128), jnp.sum(token_counts).astype(F32))]
    all_to_all x1 -> x0, local copies, waits for them, and re-layouts: 11.5 us -> none  [body(): lax.all_to_all(tokens_in, 'shard', split_axis=1, concat_axis=0, tiled=True)]
  transfers between devices with their start and end apart: 3 -> 0, of which waited for: 2 -> 0; matrix products, arithmetic and copies ran while one was open for 5% -> 0% of each run, Pallas kernels for 0% -> 0%
where the time goes in v1:
time: 244 us
  Pallas kernels  227 us (93%)
  other arithmetic  10.7 us (4%)
  local copies, waits for them, and re-layouts  3.38 us (1%)
  between operations  2.74 us (1%)
    pallas_call x1, Pallas kernels, body(): pl.pallas_call(functools.partial(kernel, dims), out_shape=(jax.ShapeDtype...  227 us
    sub x1, other arithmetic, body(): new_weight = key_weight - RATE * weight_rms * direction  6.18 us

profile of v1, /device:TPU:0, one launch (start us, length us, event | category | flops | bytes accessed | tf_op | source)
XLA Modules:
  0.0 243.6 jit_solution(9032270783990886338)
XLA Ops:
  0.6 1.3 reduce_sum.27
  2.6 1.2 slice.18
  3.8 0.6 iota_compare_fusion
  4.5 0.9 broadcast_in_dim.25.row_ref
  5.4 1.4 broadcast_select_fusion.k_ref
  6.7 0.0 copy-start.2
  6.8 226.7 %shard_map.102 = (f32[1024,1152]{1,0:T(8,128)}, f32[8,1024]{1,0:T(8,128)S(1)}) custom-call(bf16[512,8192]{1,0:T(8,128)(2,1)} %t_ref.1, bf16[512,1024]{1,0:T(8,128)(2,1)S(1)} %broadcast_select_fusion.k_ref, f32[8,128]{1,0:T(8,128)S(1)} %broadcast_in_dim.24.cnt_ref, f32[1024,1024]{1,0:T(8,128)} %acc_ref.1, f32[1024,1024]{1,0:T(8,128)} %w_ref.1, ...), custom_call_target="tpu_custom_call" | custom-call | flops 8589934592 | bytes 25165824 | tf_op jit(solution)/shard_map/pallas_call | solution.py:283
  233.5 0.6 slice_multiply_fusion
  234.8 0.0 copy-done.2
  234.8 0.6 divide_reduce_fusion
  235.4 0.0 copy-start.1
  236.1 1.2 slice_reduce_fusion
  237.4 0.0 copy-start
  237.4 6.2 %multiply_subtract_fusion = (f32[1024,1024]{1,0:T(8,128)}, f32[1024,1024]{1,0:T(8,128)}) fusion(f32[1024,1024]{1,0:T(8,128)} %w_ref.1, f32[]{:T(128)S(6)} %mul_shard_map.3, f32[]{:T(128)S(6)} %max.3, f32[1024]{0:T(1024)S(1)} %get-tuple-element.11, f32[1024]{0:T(1024)S(1)} %slice_reduce_fusion, f32[1024,1152]{1,0:T(8,128)} %get-tuple-element.7), kind=kLoop, calls=%fused_computation | loop fusion | flops 5242880 | bytes 16785416 | tf_op jit(solution)/shard_map/sub | solution.py:323
  243.6 0.0 copy-done.1
  243.6 0.0 copy-done
  (1 shorter events, 0.0 us)
Async XLA Ops:
  6.7 228.1 %copy-start.2 = (f32[1024]{0:T(1024)S(1)}, f32[1024]{0:T(1024)}, u32[]{:S(2)}) copy-start(f32[1024]{0:T(1024)} %param.13) | copy-start | bytes 12292
  235.4 8.1 %copy-start.1 = (f32[1024]{0:T(1024)}, f32[1024]{0:T(1024)S(1)}, u32[]{:S(2)}) copy-start(f32[1024]{0:T(1024)S(1)} %get-tuple-element.11) | copy-start | bytes 12292
  237.4 6.2 %copy-start = (f32[1024]{0:T(1024)}, f32[1024]{0:T(1024)S(1)}, u32[]{:S(2)}) copy-start(f32[1024]{0:T(1024)S(1)} %slice_reduce_fusion) | copy-start | bytes 12292

commit v2 on v1

--- a/solution.py
+++ b/solution.py
@@ -12,7 +12,8 @@
 CLIP = 1.0
 RATE = 0.05
 MESH = pl.DeviceIdType.MESH
-WINDOW = 3
+EARLY = 0
+WINDOW = 4
 F32 = jnp.float32
 
 
@@ -39,6 +40,9 @@
     hi, lo = shard // L, shard % L
     g0 = lo // G
 
+    def target(k):
+        return (hi + jnp.where(k == H - 1, 0, (k + H // 2 - 1) % (H - 1) + 1)) % H
+
     def dev_rep(r):
         return (r, shard)
 
@@ -66,6 +70,13 @@
     my_tok = pl.ds(pl.multiple_of(rep * tok, tok), tok)
     k_cp = pltpu.make_async_copy(k_ref, k_buf.at[my_tok], k_local.at[0])
     k_cp.start()
+    micro = cnt_ref.shape[0]
+    count = cnt_ref[0, 0]
+    for i in range(1, micro):
+        count = count + cnt_ref[i, 0]
+    k_cp.wait()
+    keep = lax.broadcasted_iota(jnp.int32, (tok, 1), 0) < cnt_ref[micro - 1, 0]
+    k_buf[my_tok, :] = jnp.where(keep, k_buf[my_tok, :], jnp.zeros((), k_buf.dtype))
     pl.semaphore_wait(barrier, len(peers))
 
     def reduce_all(first, b1, b2, b3, sends, recvs):
@@ -87,8 +98,8 @@
                 value = value + buf[i]
         return value
 
-    k_sib = rcopy(k_ref, k_buf.at[my_tok], kc_send.at[0], kc_recv.at[0], dev_rep(sib))
-    k_far = [rcopy(k_ref, k_buf.at[my_tok], kx_send.at[q - 1], kx_recv.at[q - 1],
+    k_sib = rcopy(k_buf.at[my_tok], k_buf.at[my_tok], kc_send.at[0], kc_recv.at[0], dev_rep(sib))
+    k_far = [rcopy(k_buf.at[my_tok], k_buf.at[my_tok], kx_send.at[q - 1], kx_recv.at[q - 1],
                    dev_rep(((x + q) % X) * 2 + c)) for q in range(1, X)]
     for cp in k_far:
         cp.start()
@@ -100,7 +111,7 @@
         return rcopy(k_buf.at[at], k_buf.at[at], kf_send.at[q - 1], kf_recv.at[q - 1], dev_rep(sib))
 
     def block_of(t):
-        return ((hi + 1 + t // NG) % H) * L + ((g0 + 1 + t % NG) % NG) * G
+        return target(t // NG) * L + ((g0 + 1 + t % NG) % NG) * G
 
     def t_cols(r, s0):
         if natural:
@@ -126,15 +137,16 @@
             t_rem(t, p).start()
         t_loc(t).start()
 
-    for t in range(min(WINDOW, NCH)):
+    for t in range(EARLY):
         t_start(t)
 
-    total = reduce_all(cnt_ref[...], c1, c2, c3, a_send, a_recv)
+    total = reduce_all(jnp.full((8, 128), count.astype(F32)), c1, c2, c3, a_send, a_recv)
 
     for q in range(1, X):
         k_far[q - 1].wait_recv()
         k_fwd(q).start()
-    k_cp.wait()
+    for t in range(EARLY, min(WINDOW, NCH)):
+        t_start(t)
     k_sib.wait_recv()
     for q in range(1, X):
         k_fwd(q).wait_recv()
@@ -143,15 +155,15 @@
         return pl.ds(pl.multiple_of(s * sub, n * sub), n * sub)
 
     def y_copy(k, lt, p):
-        s = ((hi + 1 + k) % H) * L + lt
+        s = target(k) * L + lt
         return rcopy(part.at[part_rows(s)], y_buf.at[p - 1, k], y_send.at[p - 1, k], y_recv.at[p - 1, k], dev_lo(lt))
 
     def z_copy(k):
-        h = (hi + 1 + k) % H
+        h = target(k)
         return rcopy(part.at[part_rows(h * L + lo)], z_buf.at[k], z_send.at[k], z_recv.at[k], dev_hi(h))
 
     def y_add(k):
-        s = ((hi + 1 + k) % H) * L + lo
+        s = target(k) * L + lo
         at = part_rows(s)
         for p in range(1, L):
             y_copy(k, (lo + p) % L, p).wait_recv()
@@ -266,10 +278,6 @@
     natural = sub % 128 == 0
     G = 1 if natural else 128 // sub
     NCH = S // G
-    live = token_counts[token_counts.shape[0] - 1, 0]
-    keep = lax.broadcasted_iota(jnp.int32, (tok, 1), 0) < live
-    masked = jnp.where(keep, key_cotangent, jnp.zeros((), key_cotangent.dtype))
-    count = jnp.full((8, 128), jnp.sum(token_counts).astype(F32))
     rows = jnp.broadcast_to(row_moment[:, None], (B, 128))
     tokens = tokens_in
     if not natural:
@@ -283,7 +291,7 @@
     grads, stats = pl.pallas_call(
         functools.partial(kernel, dims),
         out_shape=(jax.ShapeDtypeStruct((B, KV + 128), F32), jax.ShapeDtypeStruct((8, KV), F32)),
-        in_specs=[any_spec, any_spec, vmem, any_spec, any_spec, any_spec],
+        in_specs=[any_spec, any_spec, pl.BlockSpec(memory_space=pltpu.SMEM), any_spec, any_spec, any_spec],
         out_specs=(any_spec, vmem),
         scratch_shapes=[
             pltpu.VMEM((R * tok, S * sub), jnp.bfloat16),
@@ -311,7 +319,7 @@
         compiler_params=pltpu.CompilerParams(collective_id=0, has_side_effects=True,
                                              vmem_limit_bytes=50 * 1024 * 1024),
         cost_estimate=pl.CostEstimate(flops=2 * tok * D * KV, bytes_accessed=24 * 1024 * 1024, transcendentals=0),
-    )(tokens, masked, count, grad_accum, key_weight, rows)
+    )(tokens, key_cotangent, token_counts, grad_accum, key_weight, rows)
     entries = D * KV
     new_col = DECAY * col_moment + (1.0 - DECAY) * (stats[0] / D)
     update_sq = jnp.sum(stats[1] / new_col)

time: 244 us -> 214 us (0.88)
  Pallas kernels: 227 us -> 200 us
  other arithmetic: 10.7 us -> 7.4 us
    pallas_call x1, Pallas kernels: 227 us -> 200 us  [body(): pl.pallas_call(functools.partial(kernel, dims), out_shape=(jax.ShapeDtype...]
where the time goes in v2:
time: 214 us
  Pallas kernels  200 us (93%)
  other arithmetic  7.4 us (3%)
  local copies, waits for them, and re-layouts  4.1 us (2%)
    pallas_call x1, Pallas kernels, body(): pl.pallas_call(functools.partial(kernel, dims), out_shape=(jax.ShapeDtype...  200 us
    sub x1, other arithmetic, body(): new_weight = key_weight - RATE * weight_rms * direction  6.18 us

profile of v2, /device:TPU:0, one launch (start us, length us, event | category | flops | bytes accessed | tf_op | source)
XLA Modules:
  0.0 213.6 jit_solution(13177173569212217098)
XLA Ops:
  0.6 0.7 copy.12.cnt_ref
  1.4 0.9 broadcast_in_dim.2.row_ref
  2.3 0.0 copy-start
  2.3 1.2 copy-done
  3.5 0.0 copy-start.3
  3.5 200.0 %shard_map.102 = (f32[1024,1152]{1,0:T(8,128)}, f32[8,1024]{1,0:T(8,128)S(1)}) custom-call(bf16[512,8192]{1,0:T(8,128)(2,1)} %t_ref.1, bf16[512,1024]{1,0:T(8,128)(2,1)S(1)} %copy-done, s32[4,1]{1,0:T(4,128)S(1)} %copy.12.cnt_ref, f32[1024,1024]{1,0:T(8,128)} %acc_ref.1, f32[1024,1024]{1,0:T(8,128)} %w_ref.1, f32[1024,128]{1,0:T(8,128)S(1)} %broadcast_in_dim.2.row_ref), custom_call_target="tpu_custom_call" | custom-call | flops 8589934592 | bytes 25165824 | tf_op jit(solution)/shard_map/pallas_call | solution.py:291
  203.5 0.6 slice_multiply_fusion
  204.8 0.0 copy-done.3
  204.8 0.6 divide_reduce_fusion
  205.4 0.0 copy-start.2
  206.1 1.2 slice_reduce_fusion
  207.4 0.0 copy-start.1
  207.4 6.2 %multiply_subtract_fusion = (f32[1024,1024]{1,0:T(8,128)}, f32[1024,1024]{1,0:T(8,128)}) fusion(f32[1024,1024]{1,0:T(8,128)} %w_ref.1, f32[]{:T(128)S(6)} %mul_shard_map.3, f32[]{:T(128)S(6)} %max.3, f32[1024]{0:T(1024)S(1)} %get-tuple-element.11, f32[1024]{0:T(1024)S(1)} %slice_reduce_fusion, f32[1024,1152]{1,0:T(8,128)} %get-tuple-element.7), kind=kLoop, calls=%fused_computation | loop fusion | flops 5242880 | bytes 16785416 | tf_op jit(solution)/shard_map/sub | solution.py:331
  213.6 0.0 copy-done.2
  213.6 0.0 copy-done.1
Async XLA Ops:
  2.3 1.2 copy-start
  3.5 201.3 %copy-start.3 = (f32[1024]{0:T(1024)S(1)}, f32[1024]{0:T(1024)}, u32[]{:S(2)}) copy-start(f32[1024]{0:T(1024)} %param.13) | copy-start | bytes 12292
  205.4 8.1 %copy-start.2 = (f32[1024]{0:T(1024)}, f32[1024]{0:T(1024)S(1)}, u32[]{:S(2)}) copy-start(f32[1024]{0:T(1024)S(1)} %get-tuple-element.11) | copy-start | bytes 12292
  207.4 6.2 %copy-start.1 = (f32[1024]{0:T(1024)}, f32[1024]{0:T(1024)S(1)}, u32[]{:S(2)}) copy-start(f32[1024]{0:T(1024)S(1)} %slice_reduce_fusion) | copy-start | bytes 12292

commit v3 on v2

--- a/solution.py
+++ b/solution.py
@@ -14,6 +14,8 @@
 MESH = pl.DeviceIdType.MESH
 EARLY = 0
 WINDOW = 4
+PIECES = 2
+EAGER = 1
 F32 = jnp.float32
 
 
@@ -154,22 +156,35 @@
     def part_rows(s, n=1):
         return pl.ds(pl.multiple_of(s * sub, n * sub), n * sub)
 
-    def y_copy(k, lt, p):
+    piece = sub // PIECES
+
+    def piece_rows(s, e):
+        return pl.ds(pl.multiple_of(s * sub + e * piece, piece), piece)
+
+    def at_piece(e):
+        return pl.ds(e * piece, piece)
+
+    def y_copy(k, lt, p, e):
         s = target(k) * L + lt
-        return rcopy(part.at[part_rows(s)], y_buf.at[p - 1, k], y_send.at[p - 1, k], y_recv.at[p - 1, k], dev_lo(lt))
-
-    def z_copy(k):
+        return rcopy(part.at[piece_rows(s, e)], y_buf.at[p - 1, k, at_piece(e)], y_send.at[p - 1, k, e],
+                     y_recv.at[p - 1, k, e], dev_lo(lt))
+
+    def y_start(k, lt, p):
+        for e in range(PIECES):
+            y_copy(k, lt, p, e).start()
+
+    def z_copy(k, e):
         h = target(k)
-        return rcopy(part.at[part_rows(h * L + lo)], z_buf.at[k], z_send.at[k], z_recv.at[k], dev_hi(h))
-
-    def y_add(k):
-        s = target(k) * L + lo
-        at = part_rows(s)
+        return rcopy(part.at[piece_rows(h * L + lo, e)], z_buf.at[k, at_piece(e)], z_send.at[k, e],
+                     z_recv.at[k, e], dev_hi(h))
+
+    def y_add(k, e):
+        at = piece_rows(target(k) * L + lo, e)
         for p in range(1, L):
-            y_copy(k, (lo + p) % L, p).wait_recv()
+            y_copy(k, (lo + p) % L, p, e).wait_recv()
         value = part[at, :]
         for p in range(1, L):
-            value = value + y_buf[p - 1, k]
+            value = value + y_buf[p - 1, k, e * piece:(e + 1) * piece, :]
         part[at, :] = value
 
     def step(k, carry):
@@ -192,22 +207,30 @@
                 p = (lt - lo + L) % L
                 if G == 1:
                     if j < NG - 1:
-                        y_copy(k, lt, p).start()
+                        y_start(k, lt, p)
                 else:
                     @pl.when(p > 0)
                     def _():
-                        y_copy(k, lt, p).start()
+                        y_start(k, lt, p)
             if j == 0:
                 @pl.when(k > 0)
                 def _():
-                    y_add(k - 1)
-                    z_copy(k - 1).start()
+                    for e in range(EAGER, PIECES):
+                        y_add(k - 1, e)
+                        z_copy(k - 1, e).start()
+
+        @pl.when(k < H - 1)
+        def _():
+            for e in range(EAGER):
+                y_add(k, e)
+                z_copy(k, e).start()
         return carry
 
     lax.fori_loop(0, H, step, 0)
-    y_add(H - 1)
-    for k in range(H - 1):
-        z_copy(k).wait_recv()
+    for e in range(PIECES):
+        y_add(H - 1, e)
+        for k in range(H - 1):
+            z_copy(k, e).wait_recv()
     for cp in in_copies:
         cp.wait()
     value = part[part_rows(shard), :]
@@ -263,9 +286,11 @@
     lax.fori_loop(0, NCH, t_done, 0)
     for k in range(H):
         for p in range(1, L):
-            y_copy(k, (lo + p) % L, p).wait_send()
+            for e in range(PIECES):
+                y_copy(k, (lo + p) % L, p, e).wait_send()
         if k < H - 1:
-            z_copy(k).wait_send()
+            for e in range(PIECES):
+                z_copy(k, e).wait_send()
 
 
 def body(R, S, L, tokens_in, key_cotangent, token_counts, grad_accum, key_weight, row_moment, col_moment):
@@ -311,7 +336,7 @@
             pltpu.VMEM((H, 8, KV), F32),
             dma((NCH,)), dma((R - 1, NCH)), dma((R - 1, NCH)),
             dma((1,)), dma((X1,)), dma((X1,)), dma((1,)), dma((1,)), dma((X1,)), dma((X1,)),
-            dma((L - 1, H)), dma((L - 1, H)), dma((H - 1,)), dma((H - 1,)),
+            dma((L - 1, H, PIECES)), dma((L - 1, H, PIECES)), dma((H - 1, PIECES)), dma((H - 1, PIECES)),
             dma((3,)),
             dma((1,)), dma((X1,)), dma((X1,)), dma((1,)), dma((1,)), dma((X1,)), dma((X1,)),
             dma((n_all,)), dma((n_all,)), dma((n_all,)), dma((n_all,)),

time: 214 us -> 203 us (0.949)
  Pallas kernels: 200 us -> 189 us
    pallas_call x1, Pallas kernels: 200 us -> 189 us  [body(): pl.pallas_call(functools.partial(kernel, dims), out_shape=(jax.ShapeDtype...]
where the time goes in v3:
time: 203 us; the launch traced here: 202 us
  Pallas kernels  189 us (93%)
  other arithmetic  7.4 us (4%)
  local copies, waits for them, and re-layouts  4.1 us (2%)
  between operations  2.07 us (1%)
    pallas_call x1, Pallas kernels, body(): pl.pallas_call(functools.partial(kernel, dims), out_shape=(jax.ShapeDtype...  189 us
    sub x1, other arithmetic, body(): new_weight = key_weight - RATE * weight_rms * direction  6.18 us

profile of v3, /device:TPU:0, one launch (start us, length us, event | category | flops | bytes accessed | tf_op | source)
XLA Modules:
  0.0 202.4 jit_solution(771287733564808197)
XLA Ops:
  0.6 0.7 copy.12.cnt_ref
  1.4 0.9 broadcast_in_dim.2.row_ref
  2.3 0.0 copy-start
  2.3 1.2 copy-done
  3.5 0.0 copy-start.3
  3.5 188.8 %shard_map.102 = (f32[1024,1152]{1,0:T(8,128)}, f32[8,1024]{1,0:T(8,128)S(1)}) custom-call(bf16[512,8192]{1,0:T(8,128)(2,1)} %t_ref.1, bf16[512,1024]{1,0:T(8,128)(2,1)S(1)} %copy-done, s32[4,1]{1,0:T(4,128)S(1)} %copy.12.cnt_ref, f32[1024,1024]{1,0:T(8,128)} %acc_ref.1, f32[1024,1024]{1,0:T(8,128)} %w_ref.1, f32[1024,128]{1,0:T(8,128)S(1)} %broadcast_in_dim.2.row_ref), custom_call_target="tpu_custom_call" | custom-call | flops 8589934592 | bytes 25165824 | tf_op jit(solution)/shard_map/pallas_call | solution.py:316
  192.3 0.6 slice_multiply_fusion
  193.6 0.0 copy-done.3
  193.6 0.6 divide_reduce_fusion
  194.3 0.0 copy-start.2
  195.0 1.2 slice_reduce_fusion
  196.2 0.0 copy-start.1
  196.2 6.2 %multiply_subtract_fusion = (f32[1024,1024]{1,0:T(8,128)}, f32[1024,1024]{1,0:T(8,128)}) fusion(f32[1024,1024]{1,0:T(8,128)} %w_ref.1, f32[]{:T(128)S(6)} %mul_shard_map.3, f32[]{:T(128)S(6)} %max.3, f32[1024]{0:T(1024)S(1)} %get-tuple-element.11, f32[1024]{0:T(1024)S(1)} %slice_reduce_fusion, f32[1024,1152]{1,0:T(8,128)} %get-tuple-element.7), kind=kLoop, calls=%fused_computation | loop fusion | flops 5242880 | bytes 16785416 | tf_op jit(solution)/shard_map/sub | solution.py:356
  202.4 0.0 copy-done.2
  202.4 0.0 copy-done.1
Async XLA Ops:
  2.3 1.2 copy-start
  3.5 190.2 %copy-start.3 = (f32[1024]{0:T(1024)S(1)}, f32[1024]{0:T(1024)}, u32[]{:S(2)}) copy-start(f32[1024]{0:T(1024)} %param.13) | copy-start | bytes 12292
  194.3 8.1 %copy-start.2 = (f32[1024]{0:T(1024)}, f32[1024]{0:T(1024)S(1)}, u32[]{:S(2)}) copy-start(f32[1024]{0:T(1024)S(1)} %get-tuple-element.11) | copy-start | bytes 12292
  196.2 6.2 %copy-start.1 = (f32[1024]{0:T(1024)}, f32[1024]{0:T(1024)S(1)}, u32[]{:S(2)}) copy-start(f32[1024]{0:T(1024)S(1)} %slice_reduce_fusion) | copy-start | bytes 12292

commit v4 on v3

--- a/solution.py
+++ b/solution.py
@@ -14,8 +14,8 @@
 MESH = pl.DeviceIdType.MESH
 EARLY = 0
 WINDOW = 4
-PIECES = 2
-EAGER = 1
+PIECES = 4
+EAGER = 2
 F32 = jnp.float32
 
 
@@ -227,56 +227,70 @@
         return carry
 
     lax.fori_loop(0, H, step, 0)
+    for cp in in_copies:
+        cp.wait()
+    w = w_v[...]
+    wsq = jnp.sum(w * w, axis=0, keepdims=True)
+    kv = acc_v.shape[1]
+
+    def out_rows(r, e):
+        return g_out.at[pl.ds(pl.multiple_of(r * sub + e * piece, piece), piece)]
+
+    def g_cp(e):
+        return pltpu.make_async_copy(g_buf.at[at_piece(e)], out_rows(rep, e), g_local.at[e])
+
+    def g_sib(e):
+        return rcopy(g_buf.at[at_piece(e)], out_rows(rep, e), gc_send.at[e], gc_recv.at[e], dev_rep(sib))
+
+    def g_far(q, e):
+        return rcopy(g_buf.at[at_piece(e)], out_rows(rep, e), gx_send.at[q - 1, e], gx_recv.at[q - 1, e],
+                     dev_rep(((x + q) % X) * 2 + c))
+
+    def g_fwd(q, e):
+        src = ((x + X - q) % X) * 2 + c
+        return rcopy(out_rows(src, e), out_rows(src, e), gf_send.at[q - 1, e], gf_recv.at[q - 1, e], dev_rep(sib))
+
+    col = jnp.zeros((1, kv), F32)
+    upd = jnp.zeros((1, kv), F32)
     for e in range(PIECES):
         y_add(H - 1, e)
+        at = slice(e * piece, (e + 1) * piece)
+        value = part[piece_rows(shard, e), :]
         for k in range(H - 1):
             z_copy(k, e).wait_recv()
-    for cp in in_copies:
-        cp.wait()
-    value = part[part_rows(shard), :]
-    for k in range(H - 1):
-        value = value + z_buf[k]
-    grad = (acc_v[...] + value) / total[0:1, 0:1]
-    g_buf[:, :acc_v.shape[1]] = grad
-    g2 = grad * grad
-    squares = g2 + EPS
-    mean = jnp.sum(squares, axis=1, keepdims=True) / squares.shape[1]
-    new_row = DECAY * row_v[...] + (1.0 - DECAY) * mean
-    g_buf[:, acc_v.shape[1]:] = new_row
-
-    g_cp = pltpu.make_async_copy(g_buf, g_out.at[rows], g_local.at[0])
-    g_sib = rcopy(g_buf, g_out.at[rows], gc_send.at[0], gc_recv.at[0], dev_rep(sib))
-    g_far = [rcopy(g_buf, g_out.at[rows], gx_send.at[q - 1], gx_recv.at[q - 1],
-                   dev_rep(((x + q) % X) * 2 + c)) for q in range(1, X)]
-    for cp in g_far:
-        cp.start()
-    g_sib.start()
-    g_cp.start()
-
-    col = jnp.sum(squares, axis=0, keepdims=True)
-    upd = jnp.sum(g2 * (1.0 / new_row[:, :1]), axis=0, keepdims=True)
-    w = w_v[...]
-    wsq = jnp.sum(w * w, axis=0, keepdims=True)
-    stats = jnp.concatenate([col, upd, wsq, jnp.zeros((5, col.shape[1]), F32)], axis=0)
+            value = value + z_buf[k, at, :]
+        grad = (acc_v[at, :] + value) / total[0:1, 0:1]
+        g_buf[at, :kv] = grad
+        g2 = grad * grad
+        squares = g2 + EPS
+        mean = jnp.sum(squares, axis=1, keepdims=True) / kv
+        new_row = DECAY * row_v[at, :] + (1.0 - DECAY) * mean
+        g_buf[at, kv:] = new_row
+        for q in range(1, X):
+            g_far(q, e).start()
+        g_sib(e).start()
+        g_cp(e).start()
+        col = col + jnp.sum(squares, axis=0, keepdims=True)
+        upd = upd + jnp.sum(g2 * (1.0 / new_row[:, :1]), axis=0, keepdims=True)
+
+    stats = jnp.concatenate([col, upd, wsq, jnp.zeros((5, kv), F32)], axis=0)
     s_out[...] = reduce_all(stats, s1, s2, s3, b_send, b_recv)
 
-    def g_fwd(q):
-        src = ((x + X - q) % X) * 2 + c
-        at = pl.ds(pl.multiple_of(src * sub, sub), sub)
-        return rcopy(g_out.at[at], g_out.at[at], gf_send.at[q - 1], gf_recv.at[q - 1], dev_rep(sib))
-
-    for q in range(1, X):
-        g_far[q - 1].wait_recv()
-        g_fwd(q).start()
-    g_cp.wait()
-    g_sib.wait()
+    for e in range(PIECES):
+        for q in range(1, X):
+            g_far(q, e).wait_recv()
+            g_fwd(q, e).start()
+    for e in range(PIECES):
+        g_cp(e).wait()
+        g_sib(e).wait()
 
     k_sib.wait_send()
     for q in range(1, X):
         k_far[q - 1].wait_send()
         k_fwd(q).wait_send()
-        g_far[q - 1].wait_send()
-        g_fwd(q).wait()
+        for e in range(PIECES):
+            g_far(q, e).wait_send()
+            g_fwd(q, e).wait()
 
     def t_done(t, carry):
         for p in range(1, R):
@@ -338,7 +352,8 @@
             dma((1,)), dma((X1,)), dma((X1,)), dma((1,)), dma((1,)), dma((X1,)), dma((X1,)),
             dma((L - 1, H, PIECES)), dma((L - 1, H, PIECES)), dma((H - 1, PIECES)), dma((H - 1, PIECES)),
             dma((3,)),
-            dma((1,)), dma((X1,)), dma((X1,)), dma((1,)), dma((1,)), dma((X1,)), dma((X1,)),
+            dma((PIECES,)), dma((X1, PIECES)), dma((X1, PIECES)), dma((PIECES,)), dma((PIECES,)),
+            dma((X1, PIECES)), dma((X1, PIECES)),
             dma((n_all,)), dma((n_all,)), dma((n_all,)), dma((n_all,)),
         ],
         compiler_params=pltpu.CompilerParams(collective_id=0, has_side_effects=True,

time: 203 us -> 186 us (0.916)
  Pallas kernels: 189 us -> 172 us
    pallas_call x1, Pallas kernels: 189 us -> 172 us  [body(): pl.pallas_call(functools.partial(kernel, dims), out_shape=(jax.ShapeDtype...]
where the time goes in v4:
time: 186 us
  Pallas kernels  172 us (92%)
  other arithmetic  7.4 us (4%)
  local copies, waits for them, and re-layouts  4.1 us (2%)
  between operations  2.07 us (1%)
    pallas_call x1, Pallas kernels, body(): pl.pallas_call(functools.partial(kernel, dims), out_shape=(jax.ShapeDtype...  172 us
    sub x1, other arithmetic, body(): new_weight = key_weight - RATE * weight_rms * direction  6.18 us

profile of v4, /device:TPU:0, one launch (start us, length us, event | category | flops | bytes accessed | tf_op | source)
XLA Modules:
  0.0 185.9 jit_solution(14411984267168798600)
XLA Ops:
  0.6 0.7 copy.12.cnt_ref
  1.4 0.9 broadcast_in_dim.2.row_ref
  2.3 0.0 copy-start
  2.3 1.2 copy-done
  3.5 0.0 copy-start.3
  3.5 172.3 %shard_map.102 = (f32[1024,1152]{1,0:T(8,128)}, f32[8,1024]{1,0:T(8,128)S(1)}) custom-call(bf16[512,8192]{1,0:T(8,128)(2,1)} %t_ref.1, bf16[512,1024]{1,0:T(8,128)(2,1)S(1)} %copy-done, s32[4,1]{1,0:T(4,128)S(1)} %copy.12.cnt_ref, f32[1024,1024]{1,0:T(8,128)} %acc_ref.1, f32[1024,1024]{1,0:T(8,128)} %w_ref.1, f32[1024,128]{1,0:T(8,128)S(1)} %broadcast_in_dim.2.row_ref), custom_call_target="tpu_custom_call" | custom-call | flops 8589934592 | bytes 25165824 | tf_op jit(solution)/shard_map/pallas_call | solution.py:330
  175.8 0.6 slice_multiply_fusion
  177.1 0.0 copy-done.3
  177.1 0.6 divide_reduce_fusion
  177.7 0.0 copy-start.2
  178.4 1.2 slice_reduce_fusion
  179.7 0.0 copy-start.1
  179.7 6.2 %multiply_subtract_fusion = (f32[1024,1024]{1,0:T(8,128)}, f32[1024,1024]{1,0:T(8,128)}) fusion(f32[1024,1024]{1,0:T(8,128)} %w_ref.1, f32[]{:T(128)S(6)} %mul_shard_map.3, f32[]{:T(128)S(6)} %max.3, f32[1024]{0:T(1024)S(1)} %get-tuple-element.11, f32[1024]{0:T(1024)S(1)} %slice_reduce_fusion, f32[1024,1152]{1,0:T(8,128)} %get-tuple-element.7), kind=kLoop, calls=%fused_computation | loop fusion | flops 5242880 | bytes 16785416 | tf_op jit(solution)/shard_map/sub | solution.py:371
  185.9 0.0 copy-done.2
  185.9 0.0 copy-done.1
Async XLA Ops:
  2.3 1.2 copy-start
  3.5 173.6 %copy-start.3 = (f32[1024]{0:T(1024)S(1)}, f32[1024]{0:T(1024)}, u32[]{:S(2)}) copy-start(f32[1024]{0:T(1024)} %param.13) | copy-start | bytes 12292
  177.7 8.1 %copy-start.2 = (f32[1024]{0:T(1024)}, f32[1024]{0:T(1024)S(1)}, u32[]{:S(2)}) copy-start(f32[1024]{0:T(1024)S(1)} %get-tuple-element.11) | copy-start | bytes 12292
  179.7 6.2 %copy-start.1 = (f32[1024]{0:T(1024)}, f32[1024]{0:T(1024)S(1)}, u32[]{:S(2)}) copy-start(f32[1024]{0:T(1024)S(1)} %slice_reduce_fusion) | copy-start | bytes 12292
